TPU v7x, 32 devices: a whole 2x2x4 slice. The times are simulated.
32 devices in a mesh: groups: 2 (over y), tensor: 4 (over z), dp: 4 (over x, core).
Axes of the slice: x: 2, y: 2, z: 4, core: 2. Of those that a mesh axis runs over, the one named last changes fastest.
Arguments:
- hidden: bfloat16 [2, 256, 2048], P(None, ('groups', 'dp'), 'tensor'), parts along dimension 1, may hold values from -6 to 6
- attn_gain: bfloat16 [2048], replicated, may hold values from 0.25 to 1.75
- w_qkvz: bfloat16 [2048, 4, 384], P(None, 'tensor'), may hold values from -0.125 to 0.125
- w_ab: bfloat16 [2048, 4, 2], P(None, 'tensor'), may hold values from -0.125 to 0.125
- conv_weight: bfloat16 [4, 4, 256], P(None, 'tensor'), may hold values from -3 to 3
- decay_log: float32 [4], P('tensor'), may hold values from -2 to 1
- dt_bias: float32 [4], P('tensor'), may hold values from -1 to 1
- norm_gain: bfloat16 [128], replicated, may hold values from 0.25 to 1.75
- w_out: bfloat16 [512, 2048], P('tensor'), may hold values from -0.375 to 0.375
- ffn_gain: bfloat16 [2048], replicated, may hold values from 0.25 to 1.75
- w_gu: bfloat16 [2, 2048, 5120], P(None, None, 'tensor'), may hold values from -0.125 to 0.125
- w_down: bfloat16 [5120, 2048], P('tensor'), may hold values from -0.125 to 0.125
- state: float32 [256, 4, 128, 128], P(('groups', 'dp'), 'tensor'), parts along dimension 0, may hold values from -6 to 6
- conv_state: bfloat16 [256, 3, 4, 256], P(('groups', 'dp'), None, 'tensor'), parts along dimension 0, may hold values from -6 to 6
Outputs:
- next_hidden: bfloat16 [2, 256, 2048], P(None, ('groups', 'dp'), 'tensor'), parts along dimension 1
- next_state: float32 [256, 4, 128, 128], P(('groups', 'dp'), 'tensor'), parts along dimension 0
- next_conv: bfloat16 [256, 3, 4, 256], P(('groups', 'dp'), None, 'tensor'), parts along dimension 0
There are 2 independent parts, one for each index of `groups`. A program takes and returns all parts, laid end to end along the dimension named above; an argument that names none is the same for every part. Nothing has to cross between parts.
All inputs are finite; a program needn't handle non-finite values.
Results may differ from a plain program's by a relative error of at most 0.018.
Values may be sent and summed in bfloat16 or wider, within the bound.
A program may use at most 64 MiB of HBM per device.

v0:
```python
import jax
import jax.numpy as jnp
from jax import lax
from jax.sharding import PartitionSpec as P

D = 2048
HEAD = 128
STEPS = 2


norm_eps = 1e-06
highest = lax.Precision.HIGHEST


def partner_2(block, axis, stride):
    count = lax.axis_size(axis)
    route = []
    for low in range(count):
        high = low | 1 << stride
        if high != low and high < count:
            route += [(low, high), (high, low)]
    return lax.ppermute(block, axis, route)


def rounded(values):
    return lax.optimization_barrier(values.astype(jnp.bfloat16))


def rms_scaled(values, gain_vec):
    values = values.astype(jnp.float32)
    mean_square = jnp.mean(values * values, axis=-1, keepdims=True)
    return values * lax.rsqrt(mean_square + norm_eps) * gain_vec.astype(jnp.float32)


def unit_rows(values):
    return values * lax.rsqrt(jnp.sum(values * values, axis=-1, keepdims=True) + norm_eps)


def reduce_terms(partial_value):
    term_bf = rounded(partial_value)
    return lax.psum_scatter(
        term_bf.astype(jnp.float32).astype(jnp.bfloat16), "tensor", scatter_dimension=1, tiled=True
    ).astype(jnp.float32)


def on_device(
    hidden,
    attn_gain,
    w_qkvz,
    w_ab,
    conv_weight,
    decay_log,
    dt_bias,
    norm_gain,
    w_out,
    ffn_gain,
    w_gu,
    w_down,
    state,
    conv_state,
):
    seq_count = hidden.shape[1]
    rank_here = lax.axis_index("tensor")
    half_dim = HEAD // 2
    is_odd = rank_here % 2 == 1
    carried = state
    window_state = conv_state
    outputs = []
    for step_num in range(STEPS):
        own_input = hidden[step_num]
        x_full = lax.all_gather(own_input, "tensor", axis=1, tiled=True)
        normed = rms_scaled(x_full, attn_gain).astype(jnp.bfloat16)
        projected = jnp.dot(
            normed, w_qkvz.reshape(D, -1), preferred_element_type=jnp.float32
        ).reshape(seq_count, 1, 3 * HEAD)
        gate_in = jnp.dot(normed, w_ab.reshape(D, -1), preferred_element_type=jnp.float32).reshape(
            seq_count, 1, 2
        )
        mixed = rounded(projected[:, :, : 2 * HEAD])
        window = jnp.concatenate([window_state, mixed[:, None]], axis=1)
        window_state = window[:, 1:]
        conv_sum = jnp.sum(
            window.astype(jnp.float32) * conv_weight.astype(jnp.float32)[None], axis=1
        )
        conv_bf = rounded(jax.nn.silu(conv_sum))
        own_halves = conv_bf[:, 0, :HEAD]
        partner = partner_2(own_halves, "tensor", 0)
        first_part = jnp.where(is_odd, partner, own_halves)
        second_part = jnp.where(is_odd, own_halves, partner)
        query_head = jnp.concatenate(
            [first_part[:, :half_dim], second_part[:, :half_dim]], axis=1
        ).astype(jnp.float32)
        key_head = jnp.concatenate(
            [first_part[:, half_dim:], second_part[:, half_dim:]], axis=1
        ).astype(jnp.float32)
        queries = (unit_rows(query_head) * HEAD ** (-0.5))[:, None]
        key_vecs = unit_rows(key_head)[:, None]
        value_vecs = conv_bf[:, :, HEAD:].astype(jnp.float32)
        alpha = jnp.exp(-jnp.exp(decay_log) * jax.nn.softplus(gate_in[:, :, 0] + dt_bias))
        beta = jax.nn.sigmoid(gate_in[:, :, 1])
        carried = carried * alpha[:, :, None, None]
        predicted = jnp.einsum("bhk,bhkv->bhv", key_vecs, carried, precision=highest)
        delta = (value_vecs - predicted) * beta[:, :, None]
        carried = carried + key_vecs[:, :, :, None] * delta[:, :, None, :]
        core = jnp.einsum("bhk,bhkv->bhv", queries, carried, precision=highest)
        gated = (rms_scaled(core, norm_gain) * jax.nn.silu(projected[:, :, 2 * HEAD :])).astype(
            jnp.bfloat16
        )
        partial_value = jnp.dot(
            gated.reshape(seq_count, HEAD), w_out, preferred_element_type=jnp.float32
        )
        attention = reduce_terms(partial_value)
        own_mid = rounded(own_input.astype(jnp.float32) + attention)
        middle = lax.all_gather(own_mid, "tensor", axis=1, tiled=True).astype(jnp.float32)
        middle_own = own_mid.astype(jnp.float32)
        normed_mid = rms_scaled(middle, ffn_gain).astype(jnp.bfloat16)
        gate_out = jnp.dot(normed_mid, w_gu[0], preferred_element_type=jnp.float32)
        up_out = jnp.dot(normed_mid, w_gu[1], preferred_element_type=jnp.float32)
        inner = (jax.nn.silu(gate_out) * up_out).astype(jnp.bfloat16)
        feed_partial = jnp.dot(inner, w_down, preferred_element_type=jnp.float32)
        feed_own = reduce_terms(feed_partial)
        outputs.append((middle_own + feed_own).astype(jnp.bfloat16))
    return (jnp.stack(outputs), carried, window_state)


def solution(mesh):
    placed = (
        P(None, ("groups", "dp"), "tensor"),
        P(),
        P(None, "tensor", None),
        P(None, "tensor", None),
        P(None, "tensor", None),
        P("tensor"),
        P("tensor"),
        P(),
        P("tensor", None),
        P(),
        P(None, None, "tensor"),
        P("tensor", None),
        P(("groups", "dp"), "tensor", None, None),
        P(("groups", "dp"), None, "tensor", None),
    )
    return jax.shard_map(
        on_device,
        mesh=mesh,
        in_specs=placed,
        out_specs=(
            P(None, ("groups", "dp"), "tensor"),
            P(("groups", "dp"), "tensor", None, None),
            P(("groups", "dp"), None, "tensor", None),
        ),
        check_vma=False,
    )
```

profile of v0, /device:TPU:0, one launch (start us, length us, event | category | flops | bytes accessed | tf_op | source)
XLA Modules:
  0.0 170.3 jit_solution(71989505004147404)
XLA Ops:
  7.2 0.9 fusion.138
  8.1 15.2 %all-gather = bf16[1,32,2048]{2,1,0:T(8,128)(2,1)S(1)} all-gather(bf16[1,32,512]{2,1,0:T(8,128)(2,1)S(1)} %get-tuple-element.7), channel_id=2, replica_groups=mesh['groups'=2,'tensor'=4,'dp'=4] {'tensor'}, dimensions={2}, use_global_device_ids=true | all-gather | bytes 163840 | tf_op jit(solution)/shard_map/all_gather | solution.py:71
  23.5 0.7 convert_element_type.186
  24.2 0.4 fusion.38
  24.6 13.5 %all-gather.1 = bf16[1,32,2048]{2,1,0:T(8,128)(2,1)S(1)} all-gather(bf16[1,32,512]{2,1,0:T(8,128)(2,1)S(1)} %get-tuple-element.8), channel_id=3, replica_groups=mesh['groups'=2,'tensor'=4,'dp'=4] {'tensor'}, dimensions={2}, use_global_device_ids=true | all-gather | bytes 163840 | tf_op jit(solution)/shard_map/all_gather | solution.py:71
  38.2 0.4 fusion.41
  38.8 1.8 %collective-permute-start.1 = (bf16[32,128]{1,0:T(8,128)(2,1)S(1)}, bf16[32,128]{1,0:T(8,128)(2,1)S(1)}, u32[]{:S(2)}, u32[]{:S(2)}) collective-permute-start(bf16[32,128]{1,0:T(8,128)(2,1)S(1)} %slice_bitcast_fusion), channel_id=1, source_target_pairs={{0,4},{4,0},{8,12},{12,8},{1,5},{5,1},{9,13},{13,9},{2,6},{6,2},{1... | collective-permute-start | bytes 24584 | tf_op jit(solution)/shard_map/ppermute | solution.py:22
  40.6 0.3 collective-permute-start
  41.1 0.2 convolution_bitcast_fusion
  43.2 1.0 collective-permute-done
  44.7 3.5 %fusion.30 = f32[32,1,128]{2,1,0:T(1,128)S(1)} fusion(f32[32,128,1]{1,2,0:T(1,128)S(1)} %bitcast.219, f32[32,1,128,128]{3,2,1,0:T(8,128)} %param.26, f32[32]{0:T(128)S(1)} %fusion.133), kind=kOutput, calls=%fused_computation.26 | convolution fusion | flops 6815744 | bytes 2130048 | tf_op jit(solution)/shard_map/bhk,bhkv->bhv/dot_general | solution.py:102
  48.2 2.2 %fusion.26 = f32[32,1,128]{2,1,0:T(1,128)S(1)} fusion(f32[32,128,1]{1,2,0:T(1,128)S(1)} %bitcast.228, f32[32,1,128,128]{3,2,1,0:T(8,128)S(1)} %copy-done.1, f32[32]{0:T(128)S(1)} %fusion.128, f32[32,128]{1,0:T(8,128)S(1)} %multiply_bitcast_fusion.1, f32[32,128]{1,0:T(8,128)S(1)} %convert_multiply_fusion.12, f32[32]{0:T(128)S(1)} %fusion.133), kind=kOutput, calls=%fused_computation.22 | convolution fusion | flops 8388608 | bytes 2162944 | tf_op jit(solution)/shard_map/bhk,bhkv->bhv/dot_general | solution.py:102
  50.4 1.5 multiply_add_fusion
  52.2 1.0 copy-done.2
  53.3 1.9 %fusion.24 = f32[32,1,128]{2,1,0:T(1,128)S(1)} fusion(f32[32,128,1]{1,2,0:T(1,128)S(1)} %bitcast.230, f32[32,1,128,128]{3,2,1,0:T(8,128)S(1)} %multiply_add_fusion), kind=kOutput, calls=%fused_computation.20 | convolution fusion | flops 6291456 | bytes 2129920 | tf_op jit(solution)/shard_map/bhk,bhkv->bhv/dot_general | solution.py:105
  55.3 0.9 convolution_convert_fusion
  56.5 3.7 %fusion.28 = f32[32,1,128]{2,1,0:T(1,128)S(1)} fusion(f32[32,128,1]{1,2,0:T(1,128)S(1)} %bitcast.229, f32[32,1,128,128]{3,2,1,0:T(8,128)} %param.26, f32[32,128]{1,0:T(8,128)S(1)} %multiply_bitcast_fusion.1, f32[32,128]{1,0:T(8,128)S(1)} %convert_multiply_fusion.12, f32[32]{0:T(128)S(1)} %fusion.133), kind=kOutput, calls=%fused_computation.24 | convolution fusion | flops 7864320 | bytes 2162816 | tf_op jit(solution)/shard_map/bhk,bhkv->bhv/dot_general | solution.py:105
  60.3 0.9 convolution_convert_fusion.1
  61.4 14.4 %reduce-scatter.9.cloned.1.call-done = bf16[32,512]{1,0:T(8,128)(2,1)} async-done(((bf16[32,2048]{1,0:T(8,128)(2,1)}), bf16[32,512]{1,0:T(8,128)(2,1)}) %reduce-scatter.9.cloned.1.call-update) | async-done | bytes 32784 | tf_op jit(solution)/shard_map/reduce_scatter | solution.py:41
  75.8 19.7 %reduce-scatter.5.cloned.1.call-done = bf16[32,512]{1,0:T(8,128)(2,1)} async-done(((bf16[32,2048]{1,0:T(8,128)(2,1)}), bf16[32,512]{1,0:T(8,128)(2,1)}) %reduce-scatter.5.cloned.1.call-update) | async-done | bytes 32784 | tf_op jit(solution)/shard_map/reduce_scatter | solution.py:41
  95.5 0.8 fusion.81
  96.3 13.6 %all_gather.13 = bf16[32,2048]{1,0:T(8,128)(2,1)S(1)} all-gather(bf16[32,512]{1,0:T(8,128)(2,1)S(1)} %get-tuple-element.5), channel_id=1, replica_groups=mesh['groups'=2,'tensor'=4,'dp'=4] {'tensor'}, dimensions={1}, use_global_device_ids=true | all-gather | bytes 163840 | tf_op jit(solution)/shard_map/all_gather | solution.py:114
  110.0 3.5 %fusion.6 = f32[32,1280]{1,0:T(8,128)S(1)} fusion(bf16[2,2048,1280]{2,1,0:T(8,128)(2,1)} %param.24, bf16[32,2048]{1,0:T(8,128)(2,1)S(1)} %all_gather.13, f32[2048]{0:T(1024)S(1)} %convert_element_type.200, f32[32]{0:T(128)S(1)} %add_rsqrt_fusion.5), kind=kOutput, calls=%fused_computation.6 | convolution fusion | flops 168034304 | bytes 5546112 | tf_op jit(solution)/shard_map/dot_general | solution.py:117
  113.6 6.7 %convolution_convert_fusion.3 = bf16[32,2048]{1,0:T(8,128)(2,1)} fusion(bf16[1280,2048]{1,0:T(8,128)(2,1)} %param.25, bf16[2,2048,1280]{2,1,0:T(8,128)(2,1)} %param.24, f32[32,1280]{1,0:T(8,128)S(1)} %fusion.6, bf16[32,2048]{1,0:T(8,128)(2,1)S(1)} %all_gather.13, f32[2048]{0:T(1024)S(1)} %convert_element_type.200, f32[32]{0:T(128)S(1)} %add_rsqrt_fusion.5), kind=kOutput, calls=%fused_computation.19 | convolution fusion | flops 336117760 | bytes 10920064 | tf_op jit(solution)/shard_map/dot_general | solution.py:120
  120.4 13.4 %all_gather.15 = bf16[32,2048]{1,0:T(8,128)(2,1)S(1)} all-gather(bf16[32,512]{1,0:T(8,128)(2,1)S(1)} %get-tuple-element.6), channel_id=1, replica_groups=mesh['groups'=2,'tensor'=4,'dp'=4] {'tensor'}, dimensions={1}, use_global_device_ids=true | all-gather | bytes 163840 | tf_op jit(solution)/shard_map/all_gather | solution.py:114
  134.0 3.5 %fusion.4 = f32[32,1280]{1,0:T(8,128)S(1)} fusion(bf16[2,2048,1280]{2,1,0:T(8,128)(2,1)} %param.24, bf16[32,2048]{1,0:T(8,128)(2,1)S(1)} %all_gather.15, f32[32]{0:T(128)S(1)} %add_rsqrt_fusion, f32[2048]{0:T(1024)S(1)} %convert_element_type.200), kind=kOutput, calls=%fused_computation.4 | convolution fusion | flops 168034304 | bytes 5546112 | tf_op jit(solution)/shard_map/dot_general | solution.py:117
  137.5 6.7 %convolution_convert_fusion.2 = bf16[32,2048]{1,0:T(8,128)(2,1)} fusion(bf16[1280,2048]{1,0:T(8,128)(2,1)} %param.25, bf16[2,2048,1280]{2,1,0:T(8,128)(2,1)} %param.24, f32[32,1280]{1,0:T(8,128)S(1)} %fusion.4, bf16[32,2048]{1,0:T(8,128)(2,1)S(1)} %all_gather.15, f32[32]{0:T(128)S(1)} %add_rsqrt_fusion, f32[2048]{0:T(1024)S(1)} %convert_element_type.200), kind=kOutput, calls=%fused_computation.18 | convolution fusion | flops 336117760 | bytes 10920064 | tf_op jit(solution)/shard_map/dot_general | solution.py:120
  144.3 0.6 fusion.82
  144.9 0.8 fusion.94
  145.7 16.7 %reduce-scatter.11.cloned.1.call-done = bf16[32,512]{1,0:T(8,128)(2,1)} async-done(((bf16[32,2048]{1,0:T(8,128)(2,1)}), bf16[32,512]{1,0:T(8,128)(2,1)}) %reduce-scatter.11.cloned.1.call-update) | async-done | bytes 32784 | tf_op jit(solution)/shard_map/reduce_scatter | solution.py:41
  162.3 0.8 fusion.95
  163.1 0.6 pad_maximum_fusion.2
  (76 shorter events, 3.0 us)
Async XLA Ops:
  7.2 17.0 %copy-start = (bf16[2048,1,384]{2,0,1:T(8,128)(2,1)S(1)}, bf16[2048,1,384]{2,0,1:T(8,128)(2,1)}, u32[]{:S(2)}) copy-start(bf16[2048,1,384]{2,0,1:T(8,128)(2,1)} %param.16) | copy-start | bytes 4718596
  7.2 68.6 %reduce-scatter.9.cloned.1.call-start = ((), (), s32[]{:S(2)}) async-start(), calls=%async_computation.6 | async-start | bytes 163840 | tf_op jit(solution)/shard_map/reduce_scatter | solution.py:41
  8.1 30.5 %copy-start.7 = (bf16[4,1,256]{2,0,1:T(4,128)(2,1)S(1)}, bf16[4,1,256]{2,0,1:T(4,128)(2,1)}, u32[]{:S(2)}) copy-start(bf16[4,1,256]{2,0,1:T(4,128)(2,1)} %param.18) | copy-start | bytes 6148
  8.1 30.5 %copy-start.5 = (bf16[32,3,1,256]{3,0,2,1:T(8,128)(2,1)S(1)}, bf16[32,3,1,256]{3,0,2,1:T(8,128)(2,1)}, u32[]{:S(2)}) copy-start(bf16[32,3,1,256]{3,0,2,1:T(8,128)(2,1)} %param.27) | copy-start | bytes 147460
  24.2 16.7 %copy-start.8 = (bf16[2048,1,2]{0,2,1:T(2,128)(2,1)S(1)}, bf16[2048,1,2]{0,2,1:T(2,128)(2,1)}, u32[]{:S(2)}) copy-start(bf16[2048,1,2]{0,2,1:T(2,128)(2,1)} %param.17) | copy-start | bytes 24580
  24.2 18.6 %copy-start.9 = (bf16[128]{0:T(256)(128)(2,1)S(1)}, bf16[128]{0:T(256)(128)(2,1)}, u32[]{:S(2)}) copy-start(bf16[128]{0:T(256)(128)(2,1)} %param.21) | copy-start | bytes 772
  38.8 4.0 %collective-permute-start.1 = (bf16[32,128]{1,0:T(8,128)(2,1)S(1)}, bf16[32,128]{1,0:T(8,128)(2,1)S(1)}, u32[]{:S(2)}, u32[]{:S(2)}) collective-permute-start(bf16[32,128]{1,0:T(8,128)(2,1)S(1)} %slice_bitcast_fusion), channel_id=1, source_target_pairs={{0,4},{4,0},{8,12},{12,8},{1,5},{5,1},{9,13},{13,9},{2,6},{6,2},{1... | collective-permute-start | bytes 24584 | tf_op jit(solution)/shard_map/ppermute | solution.py:22
  40.6 3.7 %collective-permute-start = (bf16[32,128]{1,0:T(8,128)(2,1)S(1)}, bf16[32,128]{1,0:T(8,128)(2,1)S(1)}, u32[]{:S(2)}, u32[]{:S(2)}) collective-permute-start(bf16[32,128]{1,0:T(8,128)(2,1)S(1)} %slice_bitcast_fusion.1), channel_id=1, source_target_pairs={{0,4},{4,0},{8,12},{12,8},{1,5},{5,1},{9,13},{13,9},{2,6},{6,2},{1... | collective-permute-start | bytes 24584 | tf_op jit(solution)/shard_map/ppermute | solution.py:22
  42.8 5.5 %copy-start.1 = (f32[32,1,128,128]{3,2,1,0:T(8,128)S(1)}, f32[32,1,128,128]{3,2,1,0:T(8,128)}, u32[]{:S(2)}) copy-start(f32[32,1,128,128]{3,2,1,0:T(8,128)} %param.26) | copy-start | bytes 6291460
  51.9 1.3 copy-start.2
  51.9 3.3 %copy-start.3 = (bf16[128,2048]{1,0:T(8,128)(2,1)S(1)}, bf16[128,2048]{1,0:T(8,128)(2,1)}, u32[]{:S(2)}) copy-start(bf16[128,2048]{1,0:T(8,128)(2,1)} %param.22) | copy-start | bytes 1572868
  55.1 6.2 %copy-start.6 = (bf16[2048]{0:T(1024)(128)(2,1)S(1)}, bf16[2048]{0:T(1024)(128)(2,1)}, u32[]{:S(2)}) copy-start(bf16[2048]{0:T(1024)(128)(2,1)} %param.23) | copy-start | bytes 12292
  55.1 40.4 %copy-start.4 = (bf16[2,32,512]{2,1,0:T(8,128)(2,1)S(1)}, bf16[2,32,512]{2,1,0:T(8,128)(2,1)}, u32[]{:S(2)}) copy-start(bf16[2,32,512]{2,1,0:T(8,128)(2,1)} %param.14) | copy-start | bytes 196612
  56.2 39.3 %reduce-scatter.5.cloned.1.call-start = ((), (), s32[]{:S(2)}) async-start(), calls=%async_computation.4 | async-start | bytes 163840 | tf_op jit(solution)/shard_map/reduce_scatter | solution.py:41
  61.3 83.6 %reduce-scatter.7.cloned.1.call-start = ((), (), s32[]{:S(2)}) async-start(), calls=%async_computation.5 | async-start | bytes 163840 | tf_op jit(solution)/shard_map/reduce_scatter | solution.py:41
  120.3 42.0 %reduce-scatter.11.cloned.1.call-start = ((), (), s32[]{:S(2)}) async-start(), calls=%async_computation.7 | async-start | bytes 163840 | tf_op jit(solution)/shard_map/reduce_scatter | solution.py:41
Sparse Core Ops, SparseCore 0:
  56.3 19.4 reduce-scatter.8
  78.1 17.3 reduce-scatter.4
  120.5 17.5 reduce-scatter.6
  144.4 17.9 reduce-scatter.10
where the time goes:
time: 171 us; the launch traced here: 170 us
  blocking collectives  55.7 us (33%)
  waiting for transfers between devices  51.9 us (30%)
  matrix products  34.8 us (20%)
  between operations  15.4 us (9%)
  other arithmetic  7.94 us (5%)
  local copies, waits for them, and re-layouts  2.29 us (1%)
  starting transfers between devices  2.25 us (1%)
    reduce_scatter x4, waiting for transfers between devices, reduce_terms(): lax.psum_scatter(term_bf.astype(jnp.float32).astype(jnp.bfloat16), 'tenso...  50.8 us
    all_gather x2, blocking collectives, on_device(): x_full = lax.all_gather(own_input, 'tensor', axis=1, tiled=True)  28.7 us
    all_gather x2, blocking collectives, on_device(): lax.all_gather(own_mid, 'tensor', axis=1, tiled=True).astype(jnp.float32)  27 us
    dot_general x2, matrix products, on_device(): feed_partial = jnp.dot(inner, w_down, preferred_element_type=jnp.float32)  13.4 us
    dot_general x2, matrix products, on_device(): gate_out = jnp.dot(normed_mid, w_gu[0], preferred_element_type=jnp.float32)  7.08 us
    dot_general x2, matrix products, on_device(): jnp.einsum('bhk,bhkv->bhv', key_vecs, carried, precision=highest)  5.64 us
    dot_general x2, matrix products, on_device(): core = jnp.einsum('bhk,bhkv->bhv', queries, carried, precision=highest)  5.57 us
  transfers between devices with their start and end apart: 6, of which 4 were waited for; matrix products, arithmetic and copies ran while one was open for 10% of the time, Pallas kernels for 0%

commit v1 on v0

--- a/solution.py
+++ b/solution.py
@@ -1,6 +1,10 @@
+import functools
+
 import jax
 import jax.numpy as jnp
 from jax import lax
+from jax.experimental import pallas as pl
+from jax.experimental.pallas import tpu as pltpu
 from jax.sharding import PartitionSpec as P
 
 D = 2048
@@ -10,6 +14,7 @@
 
 norm_eps = 1e-06
 highest = lax.Precision.HIGHEST
+MESH = pl.DeviceIdType.MESH
 
 
 def partner_2(block, axis, stride):
@@ -123,6 +128,466 @@
     return (jnp.stack(outputs), carried, window_state)
 
 
+def lane_tiles_fit(mesh, width, hidden_units):
+    count = mesh.shape["tensor"]
+    return count % 2 == 0 and width % (count * 128) == 0 and hidden_units % (count * 128) == 0
+
+
+def sigmoid(values):
+    return 1.0 / (1.0 + jnp.exp(-values))
+
+
+def mixer_kernel(
+    count,
+    hidden,
+    attn_gain,
+    w_qkvz,
+    w_ab,
+    conv_weight,
+    decay_log,
+    dt_bias,
+    norm_gain,
+    w_out,
+    ffn_gain,
+    w_gu,
+    w_down,
+    state,
+    conv_state,
+    out_hidden,
+    out_state,
+    out_conv,
+    x_all,
+    qkvz,
+    ab,
+    taps,
+    out_w,
+    gu,
+    down,
+    carried,
+    window,
+    gains_in,
+    head_gain,
+    gains,
+    split_state,
+    vecs,
+    products,
+    decay,
+    half_send,
+    half_recv,
+    att_send,
+    att_recv,
+    mid_all,
+    feed_send,
+    feed_recv,
+    act,
+    hidden_out,
+    conv_out_buf,
+    local_sem,
+    x_sems,
+    half_sems,
+    att_sems,
+    mid_sems,
+    feed_sems,
+):
+    me = lax.axis_index("tensor")
+    steps, seqs, width = hidden.shape
+    rows = steps * seqs
+    units = w_down.shape[0]
+    f32, bf16 = jnp.float32, jnp.bfloat16
+
+    def peer(index):
+        pair = lax.rem(me // 2 + index // 2, count // 2)
+        return 2 * pair + lax.rem(lax.rem(me, 2) + lax.rem(index, 2), 2)
+
+    partner = peer(1)
+
+    loads = []
+
+    def load(src, dst):
+        copy = pltpu.make_async_copy(src, dst, local_sem.at[len(loads)])
+        copy.start()
+        loads.append(copy)
+        return copy
+
+    load_x = [load(hidden.at[s], x_all.at[me, pl.ds(s * seqs, seqs)]) for s in range(steps)]
+    load_gains = [load(attn_gain, gains_in.at[0]), load(ffn_gain, gains_in.at[1])]
+    load_qkvz = [load(w_qkvz, qkvz), load(w_ab, ab)]
+    load_state = load(state, carried)
+    load_conv = [load(conv_weight, taps), load(conv_state, window)]
+    load_norm = load(norm_gain, head_gain)
+    load_out = load(w_out, out_w)
+    load_gu = [load(w_gu.at[0], gu.at[0]), load(w_gu.at[1], gu.at[1])]
+    load_down = load(w_down, down)
+
+    barrier = pltpu.get_barrier_semaphore()
+    for index in range(1, count):
+        pl.semaphore_signal(
+            barrier, inc=1, device_id={"tensor": peer(index)}, device_id_type=MESH
+        )
+    pl.semaphore_wait(barrier, count - 1)
+
+    def remote(src, dst, send, recv, target):
+        return pltpu.make_async_remote_copy(
+            src_ref=src,
+            dst_ref=dst,
+            send_sem=send,
+            recv_sem=recv,
+            device_id={"tensor": target},
+            device_id_type=MESH,
+        )
+
+    for copy in load_x:
+        copy.wait()
+    sends = []
+    for index in reversed(range(1, count)):
+        copy = remote(
+            x_all.at[me], x_all.at[me], x_sems.at[0, index], x_sems.at[1, me], peer(index)
+        )
+        copy.start()
+        sends.append(copy)
+
+    for copy in load_gains:
+        copy.wait()
+    for which in range(2):
+        for part in range(count):
+            gains[which, part] = gains_in[which, :, pl.ds(part * width, width)].astype(f32)
+    load_state.wait()
+
+    @pl.loop(0, seqs)
+    def _(seq):
+        block = carried[seq]
+        high = block.astype(bf16)
+        split_state[seq, :HEAD] = high
+        split_state[seq, HEAD:] = (block - high.astype(f32)).astype(bf16)
+
+    for copy in load_qkvz:
+        copy.wait()
+
+    projected = jnp.zeros((rows, 3 * HEAD), f32)
+    gate_in = jnp.zeros((rows, 2), f32)
+    square = jnp.zeros((rows, 1), f32)
+    for index in range(count):
+        src = peer(index)
+        if index:
+            remote(
+                x_all.at[src], x_all.at[src], x_sems.at[0, index], x_sems.at[1, src], src
+            ).wait_recv()
+        block = x_all[src].astype(f32)
+        square += jnp.sum(block * block, axis=-1, keepdims=True)
+        scaled = (block * gains[0, src]).astype(bf16)
+        span = pl.ds(pl.multiple_of(src * width, width), width)
+        projected += jnp.dot(scaled, qkvz[span, :], preferred_element_type=f32)
+        gate_in += lax.dot_general(
+            scaled, ab[:, span], (((1,), (1,)), ((), ())), preferred_element_type=f32
+        )
+    factor = lax.rsqrt(square / (count * width) + norm_eps)
+    projected = projected * factor
+    gate_in = gate_in * factor
+
+    for copy in load_conv:
+        copy.wait()
+    mixed = projected[:, : 2 * HEAD].astype(bf16)
+    kept = window.shape[0]
+    for row in range(kept):
+        place = row + steps - kept
+        if place < 0:
+            conv_out_buf[row] = window[row + steps]
+        else:
+            conv_out_buf[row] = mixed[place * seqs : (place + 1) * seqs]
+    history = [window[row].astype(f32) for row in range(kept)]
+    history += [mixed[s * seqs : (s + 1) * seqs].astype(f32) for s in range(steps)]
+    tap_rows = taps[...].astype(f32)
+    conv_steps = []
+    for s in range(steps):
+        total = history[s] * tap_rows[0:1]
+        for tap in range(1, kept + 1):
+            total += history[s + tap] * tap_rows[tap : tap + 1]
+        conv_steps.append((total * sigmoid(total)).astype(bf16))
+    conv_bf = jnp.concatenate(conv_steps, axis=0)
+    half_send[...] = conv_bf[:, :HEAD]
+    half_copy = remote(
+        half_send, half_recv, half_sems.at[0], half_sems.at[1], partner
+    )
+    half_copy.start()
+    store_conv = pltpu.make_async_copy(conv_out_buf, out_conv, local_sem.at[len(loads)])
+    store_conv.start()
+
+    shift = jnp.full((rows, 1), dt_bias[0], f32)
+    rate = jnp.exp(jnp.full((rows, 1), decay_log[0], f32))
+    biased = gate_in[:, 0:1] + shift
+    softplus = jnp.maximum(biased, 0.0) + jnp.log1p(jnp.exp(-jnp.abs(biased)))
+    alpha = jnp.exp(-rate * softplus)
+    beta = sigmoid(gate_in[:, 1:2])
+    out_gate = projected[:, 2 * HEAD :]
+    out_gate = out_gate * sigmoid(out_gate)
+    value_vecs = conv_bf[:, HEAD:].astype(f32)
+    own = conv_bf[:, :HEAD].astype(f32)
+    is_odd = lax.rem(me, 2) == 1
+    low_lanes = lax.broadcasted_iota(jnp.int32, (rows, HEAD), 1) < HEAD // 2
+
+    half_copy.wait_recv()
+    other = half_recv[...].astype(f32)
+    first = jnp.where(is_odd, other, own)
+    second = jnp.where(is_odd, own, other)
+    query_raw = jnp.where(low_lanes, first, pltpu.roll(second, HEAD // 2, 1))
+    key_raw = jnp.where(low_lanes, pltpu.roll(first, HEAD // 2, 1), second)
+    query_scale = lax.rsqrt(
+        jnp.sum(query_raw * query_raw, axis=-1, keepdims=True) + norm_eps
+    ) * HEAD ** (-0.5)
+    key_scale = lax.rsqrt(jnp.sum(key_raw * key_raw, axis=-1, keepdims=True) + norm_eps)
+
+    for s in range(steps):
+        part = slice(s * seqs, (s + 1) * seqs)
+        vecs[:, 2 * s, :] = key_raw[part]
+        vecs[:, 2 * s + 1, :] = query_raw[part]
+    for row in range(2 * steps, 8):
+        vecs[:, row, :] = jnp.zeros((seqs, HEAD), f32)
+
+    group = 8
+
+    @pl.loop(0, seqs // group)
+    def _(outer):
+        for inner_seq in range(group):
+            seq = outer * group + inner_seq
+            lhs = vecs[seq].astype(bf16)
+            products[seq] = jnp.dot(
+                jnp.concatenate([lhs, lhs], axis=1),
+                split_state[seq],
+                preferred_element_type=f32,
+            )
+
+    queries = query_raw * query_scale
+    key_vecs = key_raw * key_scale
+    cut = [slice(s * seqs, (s + 1) * seqs) for s in range(steps)]
+    deltas, cores = [], []
+    total_decay = jnp.ones((seqs, 1), f32)
+    for s in range(steps):
+        a = alpha[cut[s]]
+        total_decay = total_decay * a
+        predicted = products[:, 2 * s, :] * (key_scale[cut[s]] * total_decay)
+        read = products[:, 2 * s + 1, :] * (query_scale[cut[s]] * total_decay)
+        deltas = [d * a for d in deltas]
+        for t in range(s):
+            predicted += deltas[t] * jnp.sum(
+                key_vecs[cut[s]] * key_vecs[cut[t]], axis=-1, keepdims=True
+            )
+            read += deltas[t] * jnp.sum(
+                queries[cut[s]] * key_vecs[cut[t]], axis=-1, keepdims=True
+            )
+        delta = (value_vecs[cut[s]] - predicted) * beta[cut[s]]
+        read += delta * jnp.sum(queries[cut[s]] * key_vecs[cut[s]], axis=-1, keepdims=True)
+        deltas.append(delta)
+        cores.append(read)
+    core = jnp.concatenate(cores, axis=0)
+    load_norm.wait()
+    core_factor = lax.rsqrt(jnp.mean(core * core, axis=-1, keepdims=True) + norm_eps)
+    gated = (core * core_factor * head_gain[...].astype(f32) * out_gate).astype(bf16)
+
+    load_out.wait()
+    for index in reversed(range(count)):
+        target = peer(index)
+        span = pl.ds(pl.multiple_of(target * width, width), width)
+        term = jnp.dot(gated, out_w[:, span], preferred_element_type=f32).astype(bf16)
+        if index == 0:
+            attention = term.astype(f32)
+        else:
+            att_send[index] = term
+            copy = remote(
+                att_send.at[index], att_recv.at[me], att_sems.at[0, index], att_sems.at[1, me], target
+            )
+            copy.start()
+            sends.append(copy)
+
+    decay[...] = jnp.broadcast_to(total_decay, (seqs, HEAD))
+    for s in range(steps):
+        written = deltas[s] * key_scale[cut[s]]
+        high = written.astype(bf16).astype(f32)
+        vecs[:, 4 * s // 2, :] = key_raw[cut[s]]
+        vecs[:, 4 * s // 2 + 1, :] = key_raw[cut[s]]
+        products[:, 2 * s, :] = high
+        products[:, 2 * s + 1, :] = written - high
+    for row in range(2 * steps, 8):
+        products[:, row, :] = jnp.zeros((seqs, HEAD), f32)
+
+    @pl.loop(0, seqs // group)
+    def _(outer):
+        for inner_seq in range(group):
+            seq = outer * group + inner_seq
+            columns = jnp.transpose(vecs[seq]).astype(bf16)
+            carried[seq] = carried[seq] * decay[pl.ds(seq, 1), :] + jnp.dot(
+                columns, products[seq].astype(bf16), preferred_element_type=f32
+            )
+
+    store_state = pltpu.make_async_copy(carried, out_state, local_sem.at[len(loads) + 1])
+    store_state.start()
+
+    for index in range(1, count):
+        src = peer(index)
+        remote(
+            att_send.at[index], att_recv.at[src], att_sems.at[0, index], att_sems.at[1, src], src
+        ).wait_recv()
+        attention += att_recv[src].astype(f32)
+    mid_own = (x_all[me].astype(f32) + attention).astype(bf16)
+    mid_all[me] = mid_own
+    for index in reversed(range(1, count)):
+        copy = remote(
+            mid_all.at[me], mid_all.at[me], mid_sems.at[0, index], mid_sems.at[1, me], peer(index)
+        )
+        copy.start()
+        sends.append(copy)
+
+    for copy in load_gu:
+        copy.wait()
+    square = jnp.zeros((rows, 1), f32)
+    for index in range(count):
+        src = peer(index)
+        if index:
+            remote(
+                mid_all.at[src], mid_all.at[src], mid_sems.at[0, index], mid_sems.at[1, src], src
+            ).wait_recv()
+        block = mid_all[src].astype(f32)
+        square += jnp.sum(block * block, axis=-1, keepdims=True)
+        scaled = (block * gains[1, src]).astype(bf16)
+        span = pl.ds(pl.multiple_of(src * width, width), width)
+        for which in range(2):
+            term = jnp.dot(scaled, gu[which, span, :], preferred_element_type=f32)
+            if index == 0:
+                act[which] = term
+            else:
+                act[which] += term
+    factor = lax.rsqrt(square / (count * width) + norm_eps)
+    gate_out = act[0] * factor
+    inner = (gate_out * sigmoid(gate_out) * (act[1] * factor)).astype(bf16)
+
+    load_down.wait()
+    for index in reversed(range(count)):
+        target = peer(index)
+        span = pl.ds(pl.multiple_of(target * width, width), width)
+        term = jnp.dot(inner, down[:, span], preferred_element_type=f32).astype(bf16)
+        if index == 0:
+            feed = term.astype(f32)
+        else:
+            feed_send[index] = term
+            copy = remote(
+                feed_send.at[index], feed_recv.at[me], feed_sems.at[0, index], feed_sems.at[1, me], target
+            )
+            copy.start()
+            sends.append(copy)
+    for index in range(1, count):
+        src = peer(index)
+        remote(
+            feed_send.at[index], feed_recv.at[src], feed_sems.at[0, index], feed_sems.at[1, src], src
+        ).wait_recv()
+        feed += feed_recv[src].astype(f32)
+    final = (mid_all[me].astype(f32) + feed).astype(bf16)
+    for s in range(steps):
+        hidden_out[s] = final[cut[s]]
+    store_hidden = pltpu.make_async_copy(hidden_out, out_hidden, local_sem.at[len(loads) + 2])
+    store_hidden.start()
+    half_copy.wait_send()
+    for copy in sends:
+        copy.wait_send()
+    store_conv.wait()
+    store_state.wait()
+    store_hidden.wait()
+
+
+def in_one_kernel(
+    hidden,
+    attn_gain,
+    w_qkvz,
+    w_ab,
+    conv_weight,
+    decay_log,
+    dt_bias,
+    norm_gain,
+    w_out,
+    ffn_gain,
+    w_gu,
+    w_down,
+    state,
+    conv_state,
+):
+    count = lax.axis_size("tensor")
+    steps, seqs, width = hidden.shape
+    rows, full, units = steps * seqs, count * width, w_down.shape[0]
+    kept = conv_state.shape[1]
+    f32, bf16 = jnp.float32, jnp.bfloat16
+    anywhere = pl.BlockSpec(memory_space=pl.ANY)
+    scalar = pl.BlockSpec(memory_space=pltpu.SMEM)
+    in_specs = [anywhere] * 5 + [scalar] * 2 + [anywhere] * 7
+    vmem = pltpu.VMEM
+    pair = pltpu.SemaphoreType.DMA((2, count))
+    out = pl.pallas_call(
+        functools.partial(mixer_kernel, count),
+        out_shape=(
+            jax.ShapeDtypeStruct(hidden.shape, bf16),
+            jax.ShapeDtypeStruct((seqs, HEAD, HEAD), f32),
+            jax.ShapeDtypeStruct((kept, seqs, 2 * HEAD), bf16),
+        ),
+        in_specs=in_specs,
+        out_specs=(anywhere,) * 3,
+        scratch_shapes=[
+            vmem((count, rows, width), bf16),
+            vmem((full, 3 * HEAD), bf16),
+            vmem((2, full), bf16),
+            vmem((kept + 1, 2 * HEAD), bf16),
+            vmem((HEAD, full), bf16),
+            vmem((2, full, units), bf16),
+            vmem((units, full), bf16),
+            vmem((seqs, HEAD, HEAD), f32),
+            vmem((kept, seqs, 2 * HEAD), bf16),
+            vmem((2, 1, full), bf16),
+            vmem((1, HEAD), bf16),
+            vmem((2, count, 1, width), f32),
+            vmem((seqs, 2 * HEAD, HEAD), bf16),
+            vmem((seqs, 8, HEAD), f32),
+            vmem((seqs, 8, HEAD), f32),
+            vmem((seqs, HEAD), f32),
+            vmem((rows, HEAD), bf16),
+            vmem((rows, HEAD), bf16),
+            vmem((count, rows, width), bf16),
+            vmem((count, rows, width), bf16),
+            vmem((count, rows, width), bf16),
+            vmem((count, rows, width), bf16),
+            vmem((count, rows, width), bf16),
+            vmem((2, rows, units), f32),
+            vmem(hidden.shape, bf16),
+            vmem((kept, seqs, 2 * HEAD), bf16),
+            pltpu.SemaphoreType.DMA((20,)),
+            pair,
+            pltpu.SemaphoreType.DMA((2,)),
+            pair,
+            pair,
+            pair,
+        ],
+        compiler_params=pltpu.CompilerParams(
+            collective_id=0, has_side_effects=True, vmem_limit_bytes=44 * 2**20
+        ),
+    )(
+        hidden,
+        attn_gain.reshape(1, full),
+        w_qkvz.reshape(full, 3 * HEAD),
+        w_ab.reshape(full, 2).T,
+        conv_weight.reshape(kept + 1, 2 * HEAD),
+        decay_log,
+        dt_bias,
+        norm_gain.reshape(1, HEAD),
+        w_out,
+        ffn_gain.reshape(1, full),
+        w_gu,
+        w_down,
+        state.reshape(seqs, HEAD, HEAD),
+        conv_state.reshape(seqs, kept, 2 * HEAD).transpose(1, 0, 2),
+    )
+    next_hidden, next_state, next_conv = out
+    return (
+        next_hidden,
+        next_state[:, None],
+        next_conv.transpose(1, 0, 2)[:, :, None],
+    )
+
+
 def solution(mesh):
     placed = (
         P(None, ("groups", "dp"), "tensor"),
@@ -140,14 +605,14 @@
         P(("groups", "dp"), "tensor", None, None),
         P(("groups", "dp"), None, "tensor", None),
     )
-    return jax.shard_map(
-        on_device,
-        mesh=mesh,
-        in_specs=placed,
-        out_specs=(
-            P(None, ("groups", "dp"), "tensor"),
-            P(("groups", "dp"), "tensor", None, None),
-            P(("groups", "dp"), None, "tensor", None),
-        ),
-        check_vma=False,
-    )
+    out_placed = (placed[0], placed[12], placed[13])
+
+    def whole(*args):
+        fits = lane_tiles_fit(mesh, args[0].shape[2], args[11].shape[0])
+        one_head = args[2].shape[1] == mesh.shape["tensor"]
+        body = in_one_kernel if fits and one_head else on_device
+        return jax.shard_map(
+            body, mesh=mesh, in_specs=placed, out_specs=out_placed, check_vma=False
+        )(*args)
+
+    return whole

time: 171 us -> 52.2 us (0.31)
  blocking collectives: 55.7 us -> 0 us
  waiting for transfers between devices: 51.9 us -> 0 us
  Pallas kernels: 0 us -> 38.1 us
  matrix products: 34.8 us -> 0 us
  between operations: 15.4 us -> 1.94 us
  local copies, waits for them, and re-layouts: 2.29 us -> 11.7 us
  other arithmetic: 7.94 us -> 0 us
  starting transfers between devices: 2.25 us -> 0 us
    all_gather x4 -> x0, blocking collectives: 55.7 us -> none  [the longest x2 28.7 us: on_device(): x_full = lax.all_gather(own_input, 'tensor', axis=1, tiled=True)]
    reduce_scatter x4 -> x0, waiting for transfers between devices: 50.8 us -> none  [reduce_terms(): lax.psum_scatter(term_bf.astype(jnp.float32).astype(jnp.bfloat16), 'tenso...]
    pallas_call x0 -> x1, Pallas kernels: none -> 38.1 us  [in_one_kernel(): pl.pallas_call(functools.partial(mixer_kernel, count), out_shape=(jax.Sha...]
    dot_general x14 -> x0, matrix products: 34.8 us -> none  [the longest x2 13.4 us: on_device(): feed_partial = jnp.dot(inner, w_down, preferred_element_type=jnp.float32)]
    unnamed x20 -> x19, local copies, waits for them, and re-layouts: 1.08 us -> 10.3 us
    another operation x3 -> x0, other arithmetic: 2.17 us -> none  [on_device(): return (jnp.stack(outputs), carried, window_state)]
    ppermute x2 -> x0, starting transfers between devices: 2.09 us -> none  [partner_2(): return lax.ppermute(block, axis, route)]
  transfers between devices with their start and end apart: 6 -> 0, of which waited for: 4 -> 0; matrix products, arithmetic and copies ran while one was open for 10% -> 0% of each run, Pallas kernels for 0% -> 0%
where the time goes in v1:
time: 52.2 us; the launch traced here: 51.7 us
  Pallas kernels  38.1 us (73%)
  local copies, waits for them, and re-layouts  11.7 us (22%)
  between operations  1.94 us (4%)
    pallas_call x1, Pallas kernels, in_one_kernel(): pl.pallas_call(functools.partial(mixer_kernel, count), out_shape=(jax.Sha...  38.1 us
    unnamed x19, local copies, waits for them, and re-layouts  10.3 us

profile of v1, /device:TPU:0, one launch (start us, length us, event | category | flops | bytes accessed | tf_op | source)
XLA Modules:
  0.0 51.7 jit_solution(16946719955870176225)
XLA Ops:
  1.9 0.7 %reshape.30.attn_gain = bf16[1,2048]{1,0:T(2,128)(2,1)S(1)} reshape(bf16[2048]{0:T(1024)(128)(2,1)} %param.15) | data formatting | bytes 8192 | tf_op jit(solution)/shard_map/reshape | solution.py:569
  2.6 0.7 %reshape.35.ffn_gain = bf16[1,2048]{1,0:T(2,128)(2,1)S(1)} reshape(bf16[2048]{0:T(1024)(128)(2,1)} %param.23) | data formatting | bytes 8192 | tf_op jit(solution)/shard_map/reshape | solution.py:577
  3.3 0.0 copy-start
  3.3 1.6 %copy-done = f32[32,1,128,128]{3,2,1,0:T(8,128)S(1)} copy-done((f32[32,1,128,128]{3,2,1,0:T(8,128)S(1)}, f32[32,1,128,128]{3,2,1,0:T(8,128)}, u32[]{:S(2)}) %copy-start) | copy-done | bytes 2097176
  4.9 0.0 copy-start.1
  4.9 1.4 %copy-done.1 = bf16[2048,1,384]{2,0,1:T(8,128)(2,1)S(1)} copy-done((bf16[2048,1,384]{2,0,1:T(8,128)(2,1)S(1)}, bf16[2048,1,384]{2,0,1:T(8,128)(2,1)}, u32[]{:S(2)}) %copy-start.1) | copy-done | bytes 1572888
  6.3 0.0 copy-start.2
  6.3 1.0 %copy-done.2 = bf16[128,2048]{1,0:T(8,128)(2,1)S(1)} copy-done((bf16[128,2048]{1,0:T(8,128)(2,1)S(1)}, bf16[128,2048]{1,0:T(8,128)(2,1)}, u32[]{:S(2)}) %copy-start.2) | copy-done | bytes 524312
  7.4 0.0 copy-start.3
  7.4 0.8 %copy-done.3 = bf16[2,32,512]{2,1,0:T(8,128)(2,1)S(1)} copy-done((bf16[2,32,512]{2,1,0:T(8,128)(2,1)S(1)}, bf16[2,32,512]{2,1,0:T(8,128)(2,1)}, u32[]{:S(2)}) %copy-start.3) | copy-done | bytes 65560
  8.2 0.0 copy-start.4
  8.2 0.8 %copy-done.4 = bf16[32,3,1,256]{3,0,2,1:T(8,128)(2,1)S(1)} copy-done((bf16[32,3,1,256]{3,0,2,1:T(8,128)(2,1)S(1)}, bf16[32,3,1,256]{3,0,2,1:T(8,128)(2,1)}, u32[]{:S(2)}) %copy-start.4) | copy-done | bytes 49176
  9.0 0.0 copy-start.5
  9.0 0.7 %copy-done.5 = bf16[2048,1,2]{0,2,1:T(2,128)(2,1)S(1)} copy-done((bf16[2048,1,2]{0,2,1:T(2,128)(2,1)S(1)}, bf16[2048,1,2]{0,2,1:T(2,128)(2,1)}, u32[]{:S(2)}) %copy-start.5) | copy-done | bytes 8216
  9.7 0.0 copy-start.6
  9.7 0.7 %copy-done.6 = bf16[4,1,256]{2,0,1:T(4,128)(2,1)S(1)} copy-done((bf16[4,1,256]{2,0,1:T(4,128)(2,1)S(1)}, bf16[4,1,256]{2,0,1:T(4,128)(2,1)}, u32[]{:S(2)}) %copy-start.6) | copy-done | bytes 2072
  10.4 0.0 copy-start.7
  10.4 0.7 %copy-done.7 = bf16[128]{0:T(256)(128)(2,1)S(1)} copy-done((bf16[128]{0:T(256)(128)(2,1)S(1)}, bf16[128]{0:T(256)(128)(2,1)}, u32[]{:S(2)}) %copy-start.7) | copy-done | bytes 280
  11.0 38.1 %shard_map.157 = (bf16[2,32,512]{2,1,0:T(8,128)(2,1)S(1)}, f32[32,128,128]{2,1,0:T(8,128)S(1)}, bf16[3,32,256]{2,1,0:T(8,128)(2,1)S(1)}) custom-call(bf16[2,32,512]{2,1,0:T(8,128)(2,1)S(1)} %copy-done.3, bf16[1,2048]{1,0:T(2,128)(2,1)S(1)} %reshape.30.attn_gain, bf16[2048,384]{1,0:T(8,128)(2,1)S(1)} %bitcast.20, bf16[2,2048]{1,0:T(2,128)(2,1)S(1)} %bitcast.23, ...), custom_call_target="tpu_custom_call" | custom-call | tf_op jit(solution)/shard_map/pallas_call | solution.py:521
  49.1 0.6 %copy.24 = bf16[2,32,512]{2,1,0:T(8,128)(2,1)} copy(bf16[2,32,512]{2,1,0:T(8,128)(2,1)S(1)} %get-tuple-element.15) | data formatting | bytes 131072
  49.7 1.3 %copy.25 = f32[32,1,128,128]{3,2,1,0:T(8,128)} copy(f32[32,1,128,128]{3,2,1,0:T(8,128)S(1)} %bitcast.19) | data formatting | bytes 4194304
  51.1 0.6 %copy.26 = bf16[32,3,1,256]{3,0,2,1:T(8,128)(2,1)} copy(bf16[32,3,1,256]{3,0,2,1:T(8,128)(2,1)S(1)} %bitcast.21) | data formatting | bytes 98304
Async XLA Ops:
  3.3 1.6 %copy-start = (f32[32,1,128,128]{3,2,1,0:T(8,128)S(1)}, f32[32,1,128,128]{3,2,1,0:T(8,128)}, u32[]{:S(2)}) copy-start(f32[32,1,128,128]{3,2,1,0:T(8,128)} %param.26) | copy-start | bytes 6291460
  4.9 1.4 %copy-start.1 = (bf16[2048,1,384]{2,0,1:T(8,128)(2,1)S(1)}, bf16[2048,1,384]{2,0,1:T(8,128)(2,1)}, u32[]{:S(2)}) copy-start(bf16[2048,1,384]{2,0,1:T(8,128)(2,1)} %param.16) | copy-start | bytes 4718596
  6.3 1.0 %copy-start.2 = (bf16[128,2048]{1,0:T(8,128)(2,1)S(1)}, bf16[128,2048]{1,0:T(8,128)(2,1)}, u32[]{:S(2)}) copy-start(bf16[128,2048]{1,0:T(8,128)(2,1)} %w_out.1) | copy-start | bytes 1572868
  7.4 0.8 %copy-start.3 = (bf16[2,32,512]{2,1,0:T(8,128)(2,1)S(1)}, bf16[2,32,512]{2,1,0:T(8,128)(2,1)}, u32[]{:S(2)}) copy-start(bf16[2,32,512]{2,1,0:T(8,128)(2,1)} %hidden.1) | copy-start | bytes 196612
  8.2 0.8 %copy-start.4 = (bf16[32,3,1,256]{3,0,2,1:T(8,128)(2,1)S(1)}, bf16[32,3,1,256]{3,0,2,1:T(8,128)(2,1)}, u32[]{:S(2)}) copy-start(bf16[32,3,1,256]{3,0,2,1:T(8,128)(2,1)} %param.27) | copy-start | bytes 147460
  9.0 0.7 %copy-start.5 = (bf16[2048,1,2]{0,2,1:T(2,128)(2,1)S(1)}, bf16[2048,1,2]{0,2,1:T(2,128)(2,1)}, u32[]{:S(2)}) copy-start(bf16[2048,1,2]{0,2,1:T(2,128)(2,1)} %param.17) | copy-start | bytes 24580
  9.7 0.7 %copy-start.6 = (bf16[4,1,256]{2,0,1:T(4,128)(2,1)S(1)}, bf16[4,1,256]{2,0,1:T(4,128)(2,1)}, u32[]{:S(2)}) copy-start(bf16[4,1,256]{2,0,1:T(4,128)(2,1)} %param.18) | copy-start | bytes 6148
  10.4 0.7 %copy-start.7 = (bf16[128]{0:T(256)(128)(2,1)S(1)}, bf16[128]{0:T(256)(128)(2,1)}, u32[]{:S(2)}) copy-start(bf16[128]{0:T(256)(128)(2,1)} %param.21) | copy-start | bytes 772

commit v2 on v1

--- a/solution.py
+++ b/solution.py
@@ -250,7 +250,11 @@
         copy.wait()
     for which in range(2):
         for part in range(count):
-            gains[which, part] = gains_in[which, :, pl.ds(part * width, width)].astype(f32)
+            for tile in range(width // 128):
+                row = part * (width // 128) + tile
+                gains[which, part, :, tile * 128 : (tile + 1) * 128] = gains_in[
+                    which, row : row + 1, :
+                ].astype(f32)
     load_state.wait()
 
     @pl.loop(0, seqs)
@@ -492,6 +496,23 @@
     store_hidden.wait()
 
 
+def finish_kernel(*refs):
+    sources, targets, sems = refs[:3], refs[3:6], refs[6]
+    copies = []
+    for source, target in zip(sources, targets):
+        cuts = 4 if source.shape[0] % 4 == 0 else 1
+        size = source.shape[0] // cuts
+        for cut in range(cuts):
+            span = pl.ds(cut * size, size)
+            copies.append(
+                pltpu.make_async_copy(source.at[span], target.at[span], sems.at[len(copies)])
+            )
+    for copy in copies:
+        copy.start()
+    for copy in copies:
+        copy.wait()
+
+
 def in_one_kernel(
     hidden,
     attn_gain,
@@ -515,7 +536,8 @@
     f32, bf16 = jnp.float32, jnp.bfloat16
     anywhere = pl.BlockSpec(memory_space=pl.ANY)
     scalar = pl.BlockSpec(memory_space=pltpu.SMEM)
-    in_specs = [anywhere] * 5 + [scalar] * 2 + [anywhere] * 7
+    in_hbm = pl.BlockSpec(memory_space=pltpu.HBM)
+    in_specs = [in_hbm] * 5 + [scalar] * 2 + [in_hbm] * 7
     vmem = pltpu.VMEM
     pair = pltpu.SemaphoreType.DMA((2, count))
     out = pl.pallas_call(
@@ -537,7 +559,7 @@
             vmem((units, full), bf16),
             vmem((seqs, HEAD, HEAD), f32),
             vmem((kept, seqs, 2 * HEAD), bf16),
-            vmem((2, 1, full), bf16),
+            vmem((2, full // 128, 128), bf16),
             vmem((1, HEAD), bf16),
             vmem((2, count, 1, width), f32),
             vmem((seqs, 2 * HEAD, HEAD), bf16),
@@ -562,11 +584,11 @@
             pair,
         ],
         compiler_params=pltpu.CompilerParams(
-            collective_id=0, has_side_effects=True, vmem_limit_bytes=44 * 2**20
+            collective_id=0, has_side_effects=True, vmem_limit_bytes=63 * 2**20
         ),
     )(
         hidden,
-        attn_gain.reshape(1, full),
+        attn_gain.reshape(full // 128, 128),
         w_qkvz.reshape(full, 3 * HEAD),
         w_ab.reshape(full, 2).T,
         conv_weight.reshape(kept + 1, 2 * HEAD),
@@ -574,13 +596,19 @@
         dt_bias,
         norm_gain.reshape(1, HEAD),
         w_out,
-        ffn_gain.reshape(1, full),
+        ffn_gain.reshape(full // 128, 128),
         w_gu,
         w_down,
         state.reshape(seqs, HEAD, HEAD),
         conv_state.reshape(seqs, kept, 2 * HEAD).transpose(1, 0, 2),
     )
-    next_hidden, next_state, next_conv = out
+    next_hidden, next_state, next_conv = pl.pallas_call(
+        finish_kernel,
+        out_shape=tuple(jax.ShapeDtypeStruct(a.shape, a.dtype) for a in out),
+        in_specs=[anywhere] * 3,
+        out_specs=(anywhere,) * 3,
+        scratch_shapes=[pltpu.SemaphoreType.DMA((12,))],
+    )(*out)
     return (
         next_hidden,
         next_state[:, None],

time: 52.2 us -> 107 us (2.05)
  Pallas kernels: 38.1 us -> 105 us
  local copies, waits for them, and re-layouts: 11.7 us -> 0 us
    pallas_call x0 -> x1, Pallas kernels: none -> 68.2 us  [in_one_kernel(): pl.pallas_call(finish_kernel, out_shape=tuple((jax.ShapeDtypeStruct(a.sha...]
    unnamed x19 -> x0, local copies, waits for them, and re-layouts: 10.3 us -> none
    reshape x2 -> x0, local copies, waits for them, and re-layouts: 1.39 us -> none  [the longest x1 0.69 us: in_one_kernel(): attn_gain.reshape(1, full)]
    pallas_call x1, Pallas kernels: 38.1 us -> 36.8 us  [in_one_kernel(): pl.pallas_call(functools.partial(mixer_kernel, count), out_shape=(jax.Sha...]
where the time goes in v2:
time: 107 us
  Pallas kernels  105 us (98%)
  between operations  1.93 us (2%)
    pallas_call x1, Pallas kernels, in_one_kernel(): pl.pallas_call(finish_kernel, out_shape=tuple((jax.ShapeDtypeStruct(a.sha...  68.2 us
    pallas_call x1, Pallas kernels, in_one_kernel(): pl.pallas_call(functools.partial(mixer_kernel, count), out_shape=(jax.Sha...  36.8 us

profile of v2, /device:TPU:0, one launch (start us, length us, event | category | flops | bytes accessed | tf_op | source)
XLA Modules:
  0.0 107.0 jit_solution(8317300671003036153)
XLA Ops:
  1.9 36.8 %shard_map.157 = (bf16[2,32,512]{2,1,0:T(8,128)(2,1)}, f32[32,128,128]{2,1,0:T(8,128)}, bf16[3,32,256]{2,1,0:T(8,128)(2,1)}) custom-call(bf16[2,32,512]{2,1,0:T(8,128)(2,1)} %hidden.1, bf16[16,128]{1,0:T(8,128)(2,1)} %bitcast.24, bf16[2048,384]{1,0:T(8,128)(2,1)} %bitcast.21, bf16[2,2048]{1,0:T(2,128)(2,1)} %bitcast.23, bf16[4,256]{1,0:T(4,128)(2,1)} %bitcast.26, ...), custom_call_target="tpu_custom_call" | custom-call | tf_op jit(solution)/shard_map/pallas_call | solution.py:543
  38.7 68.2 %shard_map.158 = (bf16[2,32,512]{2,1,0:T(8,128)(2,1)}, f32[32,128,128]{2,1,0:T(8,128)}, bf16[3,32,256]{2,1,0:T(8,128)(2,1)}) custom-call(bf16[2,32,512]{2,1,0:T(8,128)(2,1)} %get-tuple-element.9.refs_0_, f32[32,128,128]{2,1,0:T(8,128)} %get-tuple-element.10.refs_1_, bf16[3,32,256]{2,1,0:T(8,128)(2,1)} %get-tuple-element.11.refs_2_), custom_call_target="tpu_custom_call" | custom-call | tf_op jit(solution)/shard_map/pallas_call | solution.py:605

commit v3 on v2

--- a/solution.py
+++ b/solution.py
@@ -497,19 +497,25 @@
 
 
 def finish_kernel(*refs):
-    sources, targets, sems = refs[:3], refs[3:6], refs[6]
-    copies = []
-    for source, target in zip(sources, targets):
+    sources, targets, held, sems = refs[:3], refs[3:6], refs[6:9], refs[9]
+    inward, outward = [], []
+    for source, target, buffer in zip(sources, targets, held):
         cuts = 4 if source.shape[0] % 4 == 0 else 1
         size = source.shape[0] // cuts
         for cut in range(cuts):
-            span = pl.ds(cut * size, size)
-            copies.append(
-                pltpu.make_async_copy(source.at[span], target.at[span], sems.at[len(copies)])
-            )
-    for copy in copies:
+            span, place = pl.ds(cut * size, size), len(inward)
+            inward.append(
+                pltpu.make_async_copy(source.at[span], buffer.at[span], sems.at[0, place])
+            )
+            outward.append(
+                pltpu.make_async_copy(buffer.at[span], target.at[span], sems.at[1, place])
+            )
+    for copy in inward:
         copy.start()
-    for copy in copies:
+    for first, second in zip(inward, outward):
+        first.wait()
+        second.start()
+    for copy in outward:
         copy.wait()
 
 
@@ -607,7 +613,9 @@
         out_shape=tuple(jax.ShapeDtypeStruct(a.shape, a.dtype) for a in out),
         in_specs=[anywhere] * 3,
         out_specs=(anywhere,) * 3,
-        scratch_shapes=[pltpu.SemaphoreType.DMA((12,))],
+        scratch_shapes=[pltpu.VMEM(a.shape, a.dtype) for a in out]
+        + [pltpu.SemaphoreType.DMA((2, 12))],
+        compiler_params=pltpu.CompilerParams(vmem_limit_bytes=63 * 2**20),
     )(*out)
     return (
         next_hidden,

time: 107 us -> 41.5 us (0.39)
  Pallas kernels: 105 us -> 39.4 us
    pallas_call x1, Pallas kernels: 68.2 us -> 2.61 us  [in_one_kernel(): pl.pallas_call(finish_kernel, out_shape=tuple((jax.ShapeDtypeStruct(a.sha...]
where the time goes in v3:
time: 41.5 us; the launch traced here: 41.4 us
  Pallas kernels  39.4 us (95%)
  between operations  1.93 us (5%)
    pallas_call x1, Pallas kernels, in_one_kernel(): pl.pallas_call(functools.partial(mixer_kernel, count), out_shape=(jax.Sha...  36.8 us
    pallas_call x1, Pallas kernels, in_one_kernel(): pl.pallas_call(finish_kernel, out_shape=tuple((jax.ShapeDtypeStruct(a.sha...  2.61 us

profile of v3, /device:TPU:0, one launch (start us, length us, event | category | flops | bytes accessed | tf_op | source)
XLA Modules:
  0.0 41.4 jit_solution(17993954305706811089)
XLA Ops:
  1.9 36.8 %shard_map.157 = (bf16[2,32,512]{2,1,0:T(8,128)(2,1)}, f32[32,128,128]{2,1,0:T(8,128)}, bf16[3,32,256]{2,1,0:T(8,128)(2,1)}) custom-call(bf16[2,32,512]{2,1,0:T(8,128)(2,1)} %hidden.1, bf16[16,128]{1,0:T(8,128)(2,1)} %bitcast.24, bf16[2048,384]{1,0:T(8,128)(2,1)} %bitcast.21, bf16[2,2048]{1,0:T(2,128)(2,1)} %bitcast.23, bf16[4,256]{1,0:T(4,128)(2,1)} %bitcast.26, ...), custom_call_target="tpu_custom_call" | custom-call | tf_op jit(solution)/shard_map/pallas_call | solution.py:549
  38.7 2.6 %shard_map.158 = (bf16[2,32,512]{2,1,0:T(8,128)(2,1)}, f32[32,128,128]{2,1,0:T(8,128)}, bf16[3,32,256]{2,1,0:T(8,128)(2,1)}) custom-call(bf16[2,32,512]{2,1,0:T(8,128)(2,1)} %get-tuple-element.9.refs_0_, f32[32,128,128]{2,1,0:T(8,128)} %get-tuple-element.10.refs_1_, bf16[3,32,256]{2,1,0:T(8,128)(2,1)} %get-tuple-element.11.refs_2_), custom_call_target="tpu_custom_call" | custom-call | tf_op jit(solution)/shard_map/pallas_call | solution.py:611

commit v4 on v3

--- a/solution.py
+++ b/solution.py
@@ -130,6 +130,9 @@
 
 def lane_tiles_fit(mesh, width, hidden_units):
     count = mesh.shape["tensor"]
+    plane_count = mesh.shape["groups"] * mesh.shape["dp"]
+    if HEAD % (plane_count * 16):
+        return False
     return count % 2 == 0 and width % (count * 128) == 0 and hidden_units % (count * 128) == 0
 
 
@@ -139,6 +142,7 @@
 
 def mixer_kernel(
     count,
+    planes,
     hidden,
     attn_gain,
     w_qkvz,
@@ -174,8 +178,8 @@
     decay,
     half_send,
     half_recv,
-    att_send,
-    att_recv,
+    gated_all,
+    w_peers,
     mid_all,
     feed_send,
     feed_recv,
@@ -185,7 +189,9 @@
     local_sem,
     x_sems,
     half_sems,
-    att_sems,
+    gated_sems,
+    w_sems,
+    plane_sems,
     mid_sems,
     feed_sems,
 ):
@@ -200,6 +206,20 @@
         return 2 * pair + lax.rem(lax.rem(me, 2) + lax.rem(index, 2), 2)
 
     partner = peer(1)
+    per_group = planes[1]
+    plane_count = planes[0] * planes[1]
+    here = lax.axis_index("groups") * per_group + lax.axis_index("dp")
+    piece = HEAD // plane_count
+    own_rows = pl.ds(pl.multiple_of(here * piece, piece), piece)
+
+    def columns_of(index):
+        return pl.ds(pl.multiple_of(index * width, width), width)
+
+    def plane_peer(offset):
+        return lax.rem(here + offset, plane_count)
+
+    def plane_id(place):
+        return {"groups": place // per_group, "dp": lax.rem(place, per_group)}
 
     loads = []
 
@@ -215,7 +235,7 @@
     load_state = load(state, carried)
     load_conv = [load(conv_weight, taps), load(conv_state, window)]
     load_norm = load(norm_gain, head_gain)
-    load_out = load(w_out, out_w)
+    load_out = load(w_out.at[:, columns_of(me)], out_w)
     load_gu = [load(w_gu.at[0], gu.at[0]), load(w_gu.at[1], gu.at[1])]
     load_down = load(w_down, down)
 
@@ -224,7 +244,11 @@
         pl.semaphore_signal(
             barrier, inc=1, device_id={"tensor": peer(index)}, device_id_type=MESH
         )
-    pl.semaphore_wait(barrier, count - 1)
+    for offset in range(1, plane_count):
+        pl.semaphore_signal(
+            barrier, inc=1, device_id=plane_id(plane_peer(offset)), device_id_type=MESH
+        )
+    pl.semaphore_wait(barrier, count - 1 + plane_count - 1)
 
     def remote(src, dst, send, recv, target):
         return pltpu.make_async_remote_copy(
@@ -232,7 +256,7 @@
             dst_ref=dst,
             send_sem=send,
             recv_sem=recv,
-            device_id={"tensor": target},
+            device_id=target if isinstance(target, dict) else {"tensor": target},
             device_id_type=MESH,
         )
 
@@ -242,6 +266,19 @@
     for index in reversed(range(1, count)):
         copy = remote(
             x_all.at[me], x_all.at[me], x_sems.at[0, index], x_sems.at[1, me], peer(index)
+        )
+        copy.start()
+        sends.append(copy)
+
+    half = count // 2
+    for index in range(1, count):
+        slot = 2 * ((half - index // 2) % half) + index % 2 - 1
+        copy = remote(
+            w_out.at[own_rows, columns_of(peer(index))],
+            w_peers.at[here, slot],
+            w_sems.at[0, index],
+            w_sems.at[1, slot + 1],
+            peer(index),
         )
         copy.start()
         sends.append(copy)
@@ -272,6 +309,25 @@
     square = jnp.zeros((rows, 1), f32)
     for index in range(count):
         src = peer(index)
+        if index == count - 1:
+            for slot in range(count - 1):
+                remote(
+                    w_peers.at[here, slot],
+                    w_peers.at[here, slot],
+                    w_sems.at[0, slot + 1],
+                    w_sems.at[1, slot + 1],
+                    peer(slot + 1),
+                ).wait_recv()
+            for offset in range(1, plane_count):
+                copy = remote(
+                    w_peers.at[here],
+                    w_peers.at[here],
+                    plane_sems.at[0, offset],
+                    plane_sems.at[1, here],
+                    plane_id(plane_peer(offset)),
+                )
+                copy.start()
+                sends.append(copy)
         if index:
             remote(
                 x_all.at[src], x_all.at[src], x_sems.at[0, index], x_sems.at[1, src], src
@@ -387,20 +443,13 @@
     core_factor = lax.rsqrt(jnp.mean(core * core, axis=-1, keepdims=True) + norm_eps)
     gated = (core * core_factor * head_gain[...].astype(f32) * out_gate).astype(bf16)
 
-    load_out.wait()
-    for index in reversed(range(count)):
-        target = peer(index)
-        span = pl.ds(pl.multiple_of(target * width, width), width)
-        term = jnp.dot(gated, out_w[:, span], preferred_element_type=f32).astype(bf16)
-        if index == 0:
-            attention = term.astype(f32)
-        else:
-            att_send[index] = term
-            copy = remote(
-                att_send.at[index], att_recv.at[me], att_sems.at[0, index], att_sems.at[1, me], target
-            )
-            copy.start()
-            sends.append(copy)
+    gated_all[me] = gated
+    for index in reversed(range(1, count)):
+        copy = remote(
+            gated_all.at[me], gated_all.at[me], gated_sems.at[0, index], gated_sems.at[1, me], peer(index)
+        )
+        copy.start()
+        sends.append(copy)
 
     decay[...] = jnp.broadcast_to(total_decay, (seqs, HEAD))
     for s in range(steps):
@@ -425,12 +474,25 @@
     store_state = pltpu.make_async_copy(carried, out_state, local_sem.at[len(loads) + 1])
     store_state.start()
 
+    load_out.wait()
+    attention = jnp.dot(gated, out_w[...], preferred_element_type=f32).astype(bf16).astype(f32)
+    for offset in range(1, plane_count):
+        place = plane_peer(offset)
+        remote(
+            w_peers.at[place],
+            w_peers.at[place],
+            plane_sems.at[0, offset],
+            plane_sems.at[1, place],
+            plane_id(place),
+        ).wait_recv()
     for index in range(1, count):
         src = peer(index)
         remote(
-            att_send.at[index], att_recv.at[src], att_sems.at[0, index], att_sems.at[1, src], src
+            gated_all.at[src], gated_all.at[src], gated_sems.at[0, index], gated_sems.at[1, src], src
         ).wait_recv()
-        attention += att_recv[src].astype(f32)
+        weight = w_peers[:, index - 1].reshape(HEAD, width)
+        term = jnp.dot(gated_all[src], weight, preferred_element_type=f32)
+        attention += term.astype(bf16).astype(f32)
     mid_own = (x_all[me].astype(f32) + attention).astype(bf16)
     mid_all[me] = mid_own
     for index in reversed(range(1, count)):
@@ -539,6 +601,8 @@
     steps, seqs, width = hidden.shape
     rows, full, units = steps * seqs, count * width, w_down.shape[0]
     kept = conv_state.shape[1]
+    planes = (lax.axis_size("groups"), lax.axis_size("dp"))
+    plane_count = planes[0] * planes[1]
     f32, bf16 = jnp.float32, jnp.bfloat16
     anywhere = pl.BlockSpec(memory_space=pl.ANY)
     scalar = pl.BlockSpec(memory_space=pltpu.SMEM)
@@ -547,7 +611,7 @@
     vmem = pltpu.VMEM
     pair = pltpu.SemaphoreType.DMA((2, count))
     out = pl.pallas_call(
-        functools.partial(mixer_kernel, count),
+        functools.partial(mixer_kernel, count, planes),
         out_shape=(
             jax.ShapeDtypeStruct(hidden.shape, bf16),
             jax.ShapeDtypeStruct((seqs, HEAD, HEAD), f32),
@@ -560,7 +624,7 @@
             vmem((full, 3 * HEAD), bf16),
             vmem((2, full), bf16),
             vmem((kept + 1, 2 * HEAD), bf16),
-            vmem((HEAD, full), bf16),
+            vmem((HEAD, width), bf16),
             vmem((2, full, units), bf16),
             vmem((units, full), bf16),
             vmem((seqs, HEAD, HEAD), f32),
@@ -574,8 +638,8 @@
             vmem((seqs, HEAD), f32),
             vmem((rows, HEAD), bf16),
             vmem((rows, HEAD), bf16),
-            vmem((count, rows, width), bf16),
-            vmem((count, rows, width), bf16),
+            vmem((count, rows, HEAD), bf16),
+            vmem((plane_count, count - 1, HEAD // plane_count, width), bf16),
             vmem((count, rows, width), bf16),
             vmem((count, rows, width), bf16),
             vmem((count, rows, width), bf16),
@@ -586,6 +650,8 @@
             pair,
             pltpu.SemaphoreType.DMA((2,)),
             pair,
+            pair,
+            pltpu.SemaphoreType.DMA((2, plane_count)),
             pair,
             pair,
         ],

time: 41.5 us -> 41.3 us (level)
  no operation moved by 1% of the time
where the time goes in v4:
time: 41.3 us; the launch traced here: 41.1 us
  Pallas kernels  39.2 us (95%)
  between operations  1.93 us (5%)
    pallas_call x1, Pallas kernels, in_one_kernel(): pl.pallas_call(functools.partial(mixer_kernel, count, planes), out_shape=...  36.6 us
    pallas_call x1, Pallas kernels, in_one_kernel(): pl.pallas_call(finish_kernel, out_shape=tuple((jax.ShapeDtypeStruct(a.sha...  2.61 us

profile of v4, /device:TPU:0, one launch (start us, length us, event | category | flops | bytes accessed | tf_op | source)
XLA Modules:
  0.0 41.1 jit_solution(650471484438637364)
XLA Ops:
  1.9 36.6 %shard_map.157 = (bf16[2,32,512]{2,1,0:T(8,128)(2,1)}, f32[32,128,128]{2,1,0:T(8,128)}, bf16[3,32,256]{2,1,0:T(8,128)(2,1)}) custom-call(bf16[2,32,512]{2,1,0:T(8,128)(2,1)} %hidden.1, bf16[16,128]{1,0:T(8,128)(2,1)} %bitcast.24, bf16[2048,384]{1,0:T(8,128)(2,1)} %bitcast.21, bf16[2,2048]{1,0:T(2,128)(2,1)} %bitcast.23, bf16[4,256]{1,0:T(4,128)(2,1)} %bitcast.26, ...), custom_call_target="tpu_custom_call" | custom-call | tf_op jit(solution)/shard_map/pallas_call | solution.py:613
  38.5 2.6 %shard_map.158 = (bf16[2,32,512]{2,1,0:T(8,128)(2,1)}, f32[32,128,128]{2,1,0:T(8,128)}, bf16[3,32,256]{2,1,0:T(8,128)(2,1)}) custom-call(bf16[2,32,512]{2,1,0:T(8,128)(2,1)} %get-tuple-element.9.refs_0_, f32[32,128,128]{2,1,0:T(8,128)} %get-tuple-element.10.refs_1_, bf16[3,32,256]{2,1,0:T(8,128)(2,1)} %get-tuple-element.11.refs_2_), custom_call_target="tpu_custom_call" | custom-call | tf_op jit(solution)/shard_map/pallas_call | solution.py:677

commit v5 on v4

--- a/solution.py
+++ b/solution.py
@@ -263,7 +263,7 @@
     for copy in load_x:
         copy.wait()
     sends = []
-    for index in reversed(range(1, count)):
+    for index in range(1, count):
         copy = remote(
             x_all.at[me], x_all.at[me], x_sems.at[0, index], x_sems.at[1, me], peer(index)
         )
@@ -444,7 +444,7 @@
     gated = (core * core_factor * head_gain[...].astype(f32) * out_gate).astype(bf16)
 
     gated_all[me] = gated
-    for index in reversed(range(1, count)):
+    for index in range(1, count):
         copy = remote(
             gated_all.at[me], gated_all.at[me], gated_sems.at[0, index], gated_sems.at[1, me], peer(index)
         )
@@ -495,7 +495,7 @@
         attention += term.astype(bf16).astype(f32)
     mid_own = (x_all[me].astype(f32) + attention).astype(bf16)
     mid_all[me] = mid_own
-    for index in reversed(range(1, count)):
+    for index in range(1, count):
         copy = remote(
             mid_all.at[me], mid_all.at[me], mid_sems.at[0, index], mid_sems.at[1, me], peer(index)
         )

time: 41.3 us -> 40.4 us (0.978)
  Pallas kernels: 39.2 us -> 38.3 us
    pallas_call x1, Pallas kernels: 36.6 us -> 35.6 us  [in_one_kernel(): pl.pallas_call(functools.partial(mixer_kernel, count, planes), out_shape=...]
where the time goes in v5:
time: 40.4 us; the launch traced here: 40.2 us
  Pallas kernels  38.3 us (95%)
  between operations  1.93 us (5%)
    pallas_call x1, Pallas kernels, in_one_kernel(): pl.pallas_call(functools.partial(mixer_kernel, count, planes), out_shape=...  35.6 us
    pallas_call x1, Pallas kernels, in_one_kernel(): pl.pallas_call(finish_kernel, out_shape=tuple((jax.ShapeDtypeStruct(a.sha...  2.61 us

profile of v5, /device:TPU:0, one launch (start us, length us, event | category | flops | bytes accessed | tf_op | source)
XLA Modules:
  0.0 40.2 jit_solution(4725573264034031207)
XLA Ops:
  1.9 35.6 %shard_map.157 = (bf16[2,32,512]{2,1,0:T(8,128)(2,1)}, f32[32,128,128]{2,1,0:T(8,128)}, bf16[3,32,256]{2,1,0:T(8,128)(2,1)}) custom-call(bf16[2,32,512]{2,1,0:T(8,128)(2,1)} %hidden.1, bf16[16,128]{1,0:T(8,128)(2,1)} %bitcast.24, bf16[2048,384]{1,0:T(8,128)(2,1)} %bitcast.21, bf16[2,2048]{1,0:T(2,128)(2,1)} %bitcast.23, bf16[4,256]{1,0:T(4,128)(2,1)} %bitcast.26, ...), custom_call_target="tpu_custom_call" | custom-call | tf_op jit(solution)/shard_map/pallas_call | solution.py:613
  37.6 2.6 %shard_map.158 = (bf16[2,32,512]{2,1,0:T(8,128)(2,1)}, f32[32,128,128]{2,1,0:T(8,128)}, bf16[3,32,256]{2,1,0:T(8,128)(2,1)}) custom-call(bf16[2,32,512]{2,1,0:T(8,128)(2,1)} %get-tuple-element.9.refs_0_, f32[32,128,128]{2,1,0:T(8,128)} %get-tuple-element.10.refs_1_, bf16[3,32,256]{2,1,0:T(8,128)(2,1)} %get-tuple-element.11.refs_2_), custom_call_target="tpu_custom_call" | custom-call | tf_op jit(solution)/shard_map/pallas_call | solution.py:677
